TPU v7x, 32 devices: a whole 2x2x4 slice. The times are simulated.
32 devices in a mesh: rep: 4 (over z), shard: 8 (over y, x, core).
Axes of the slice: x: 2, y: 2, z: 4, core: 2. Of those that a mesh axis runs over, the one named last changes fastest.
Arguments:
- tokens: bfloat16 [4096, 2048], P(('rep', 'shard')), may hold values from -6 to 6
- norm_gains: bfloat16 [4, 2048], P(None, 'shard'), may hold values from 0.5 to 1.5
- w_qkv: bfloat16 [2048, 6144], P('shard'), may hold values from -0.125 to 0.125
- w_attn_out: bfloat16 [2048, 2048], P('shard'), may hold values from -0.5 to 0.5
- w_in: bfloat16 [16, 2048, 2048], P(None, 'shard'), may hold values from -0.125 to 0.125
- w_out: bfloat16 [16, 2048, 1024], P(None, 'shard'), may hold values from -0.75 to 0.75
- route_gates: float32 [4096, 8], P(('rep', 'shard')), may hold values from 0.06 to 0.2
- routes: int32 [4096, 8], P(('rep', 'shard')), may hold values from 0 to 15, all different within a row; in each aligned block of 128 rows (0 to 127, 128 to 255, ...) at most 72 rows name the same one
- prefix: int32 [32], P(('rep', 'shard')), may hold values from 12 to 64
- cotangent: bfloat16 [4096, 2048], P(('rep', 'shard')), may hold values from -6 to 6
Outputs:
- layer_out: bfloat16 [4096, 2048], P(('rep', 'shard'))
- tokens_grad: bfloat16 [4096, 2048], P(('rep', 'shard'))
- gains_grad: float32 [4, 2048], P(None, 'shard')
- qkv_grad: float32 [2048, 6144], P('shard')
- attn_out_grad: float32 [2048, 2048], P('shard')
- in_grad: float32 [16, 2048, 2048], P(None, 'shard')
- out_grad: float32 [16, 2048, 1024], P(None, 'shard')
Inputs may be any that keep to these rules, and one draw needn't show every extreme that they name: `routes`: each row names 8 different experts; among the rows of one device no expert is named more than 72 times, a bound that some block reaches.
All inputs are finite; a program needn't handle non-finite values.
Results may differ from a plain program's by a relative error of at most 0.02.
Values may be sent and summed in bfloat16 or wider, within the bound.
No kernel may reach another device: no remote copies, remote signals or barrier semaphores. Data moves between devices by JAX's collectives and lax.ppermute only.
A program may use at most 320 MiB of HBM per device.

v0:
```python
import math

import jax
import jax.numpy as jnp
from jax import lax
from jax.sharding import PartitionSpec as P

D = 2048
HEADS = 16
HEAD_DIM = 128
FF = 1024
EXPERTS = 16
TOPK = 8
CAP = 72


epsilon = 1e-05
masked_value = -1e30


def norm_parts(vector):
    inverse = lax.rsqrt(jnp.mean(vector * vector, axis=-1, keepdims=True) + epsilon)
    return (vector * inverse, inverse)


def norm_back(upstream, unit_rows, inverse):
    return inverse * (upstream - unit_rows * jnp.mean(upstream * unit_rows, axis=-1, keepdims=True))


def rotate(vector, direction):
    length = vector.shape[0]
    halfway = vector.shape[-1] // 2
    frequency = 10000.0 ** (-jnp.arange(halfway, dtype=jnp.float32) / halfway)
    angles = jnp.arange(length, dtype=jnp.float32)[:, None] * frequency[None, :]
    cosine = jnp.cos(angles)[:, None, :]
    sine_part = direction * jnp.sin(angles)[:, None, :]
    first_half = vector[..., :halfway]
    second_half = vector[..., halfway:]
    return jnp.concatenate(
        [
            first_half * cosine - second_half * sine_part,
            second_half * cosine + first_half * sine_part,
        ],
        axis=-1,
    )


def dispatch(routes, route_gates):
    length = routes.shape[0]
    flat_routes = routes.reshape(-1)
    onehot = (flat_routes[:, None] == jnp.arange(EXPERTS, dtype=jnp.int32)[None, :]).astype(
        jnp.int32
    )
    before = jnp.cumsum(onehot, axis=0) - onehot
    in_expert = jnp.sum(before * onehot, axis=1)
    assign_slot = flat_routes * CAP + in_expert
    token_index = jnp.arange(length * TOPK, dtype=jnp.int32) // TOPK
    slot_token = jnp.zeros((EXPERTS * CAP,), jnp.int32).at[assign_slot].set(token_index)
    slot_live = jnp.zeros((EXPERTS * CAP,), jnp.bool_).at[assign_slot].set(True)
    slot_gate = (
        jnp.zeros((EXPERTS * CAP,), jnp.float32).at[assign_slot].set(route_gates.reshape(-1))
    )
    return (slot_token, slot_live, assign_slot, slot_gate)


def expert_forward(slot_rows, weight_in, weight_out):
    gate_up = jnp.einsum("erd,edf->erf", slot_rows, weight_in, preferred_element_type=jnp.float32)
    gate_part = gate_up[..., :FF]
    hidden = (gate_part * jax.nn.sigmoid(gate_part) * gate_up[..., FF:]).astype(jnp.bfloat16)
    result = jnp.einsum(
        "erf,edf->erd", hidden, weight_out, preferred_element_type=jnp.float32
    ).astype(jnp.bfloat16)
    return (gate_up, result)


def expert_backward(slot_rows, gate_up, upstream, weight_in, weight_out):
    gate_part = gate_up[..., :FF]
    up_part = gate_up[..., FF:]
    sigmoid_gate = jax.nn.sigmoid(gate_part)
    silu_gate = gate_part * sigmoid_gate
    hidden = (silu_gate * up_part).astype(jnp.bfloat16)
    grad_hidden = jnp.einsum(
        "erd,edf->erf", upstream, weight_out, preferred_element_type=jnp.float32
    )
    grad_out = jnp.einsum("erd,erf->edf", upstream, hidden, preferred_element_type=jnp.float32)
    grad_gate = grad_hidden * up_part * sigmoid_gate * (1.0 + gate_part * (1.0 - sigmoid_gate))
    grad_up = grad_hidden * silu_gate
    grad_gate_up = jnp.concatenate([grad_gate, grad_up], axis=-1).astype(jnp.bfloat16)
    grad_rows = jnp.einsum(
        "erf,edf->erd", grad_gate_up, weight_in, preferred_element_type=jnp.float32
    ).astype(jnp.bfloat16)
    grad_in = jnp.einsum(
        "erd,erf->edf", slot_rows, grad_gate_up, preferred_element_type=jnp.float32
    )
    return (grad_rows, grad_in, grad_out)


def attention_scores(queries, key_rows, allowed, score_scale):
    scores = (
        jnp.einsum("qhd,khd->hqk", queries, key_rows, preferred_element_type=jnp.float32)
        * score_scale
    )
    return jnp.where(allowed[None], scores, masked_value)


def body(
    tokens, norm_gains, w_qkv, w_attn_out, w_in, w_out, route_gates, routes, prefix, cotangent
):
    length = tokens.shape[0]
    score_scale = 1.0 / math.sqrt(HEAD_DIM)
    gains_full, qkv_full, attn_out_full = (
        lax.all_gather(norm_gains, "shard", axis=1, tiled=True),
        lax.all_gather(w_qkv, "shard", axis=0, tiled=True),
        lax.all_gather(w_attn_out, "shard", axis=0, tiled=True),
    )
    inputs = tokens.astype(jnp.float32)
    unit_first, inverse_first = norm_parts(inputs)
    normed = (unit_first * gains_full[0]).astype(jnp.bfloat16)
    project = jnp.dot(normed, qkv_full, preferred_element_type=jnp.float32)
    unit_query, inverse_query = norm_parts(project[:, :D])
    unit_keys, inverse_keys = norm_parts(project[:, D : 2 * D])
    queries = rotate((unit_query * gains_full[1]).reshape(length, HEADS, HEAD_DIM), 1.0).astype(
        jnp.bfloat16
    )
    key_rows = rotate((unit_keys * gains_full[2]).reshape(length, HEADS, HEAD_DIM), 1.0).astype(
        jnp.bfloat16
    )
    values = project[:, 2 * D :].astype(jnp.bfloat16).reshape(length, HEADS, HEAD_DIM)
    positions = jnp.arange(length, dtype=jnp.int32)
    allowed = (positions[None, :] <= positions[:, None]) | (positions[None, :] < prefix[0])
    masked = attention_scores(queries, key_rows, allowed, score_scale)
    top_score = jnp.max(masked, axis=-1, keepdims=True)
    log_total = top_score + jnp.log(jnp.sum(jnp.exp(masked - top_score), axis=-1, keepdims=True))
    attn_probs = jnp.exp(masked - log_total).astype(jnp.bfloat16)
    attended = (
        jnp.einsum("hqk,khd->qhd", attn_probs, values, preferred_element_type=jnp.float32)
        .reshape(length, D)
        .astype(jnp.bfloat16)
    )
    branch = jnp.dot(attended, attn_out_full, preferred_element_type=jnp.float32)
    middle = inputs + branch
    unit_second, inverse_second = norm_parts(middle)
    normed_ffn = (unit_second * gains_full[3]).astype(jnp.bfloat16)
    slot_token, slot_live, assign_slot, slot_gate = dispatch(routes, route_gates)
    expert_in = jnp.where(
        slot_live[:, None], normed_ffn[slot_token], jnp.zeros((), jnp.bfloat16)
    ).reshape(EXPERTS, CAP, D)
    owned_in, owned_out = (
        lax.all_to_all(w_in, "shard", split_axis=0, concat_axis=1, tiled=True),
        lax.all_to_all(w_out, "shard", split_axis=0, concat_axis=1, tiled=True),
    )
    arrived = lax.all_to_all(expert_in, "shard", split_axis=0, concat_axis=1, tiled=True)
    kept_gate_up, result = expert_forward(arrived, owned_in, owned_out)
    expert_out = lax.all_to_all(result, "shard", split_axis=1, concat_axis=0, tiled=True)
    picked = (
        expert_out.reshape(EXPERTS * CAP, D)[assign_slot]
        .reshape(length, TOPK, D)
        .astype(jnp.float32)
    )
    expert_mix = jnp.sum(picked * route_gates[:, :, None], axis=1)
    output = (middle + expert_mix).astype(jnp.bfloat16)
    upstream = cotangent.astype(jnp.float32)
    grad_slots = (
        (upstream[slot_token] * slot_gate[:, None]).astype(jnp.bfloat16).reshape(EXPERTS, CAP, D)
    )
    arrived_grads = lax.all_to_all(grad_slots, "shard", split_axis=0, concat_axis=1, tiled=True)
    grad_rows, grad_in, grad_out = expert_backward(
        arrived, kept_gate_up, arrived_grads, owned_in, owned_out
    )
    grad_expert_in = lax.all_to_all(grad_rows, "shard", split_axis=1, concat_axis=0, tiled=True)
    in_grads, out_grads = (
        lax.all_to_all(
            grad_in.astype(jnp.bfloat16), "shard", split_axis=1, concat_axis=0, tiled=True
        ).astype(grad_in.dtype),
        lax.all_to_all(
            grad_out.astype(jnp.bfloat16), "shard", split_axis=1, concat_axis=0, tiled=True
        ).astype(grad_out.dtype),
    )
    grad_normed_ffn = jnp.sum(
        grad_expert_in.reshape(EXPERTS * CAP, D)[assign_slot]
        .reshape(length, TOPK, D)
        .astype(jnp.float32),
        axis=1,
    )
    gains_back, qkv_back, attn_out_back = (
        lax.all_gather(norm_gains, "shard", axis=1, tiled=True),
        lax.all_gather(w_qkv, "shard", axis=0, tiled=True),
        lax.all_gather(w_attn_out, "shard", axis=0, tiled=True),
    )
    grad_gain_ffn = jnp.sum(grad_normed_ffn * unit_second, axis=0)
    grad_middle = upstream + norm_back(grad_normed_ffn * gains_back[3], unit_second, inverse_second)
    grad_branch = grad_middle.astype(jnp.bfloat16)
    grad_attended = (
        jnp.einsum("sb,ab->sa", grad_branch, attn_out_back, preferred_element_type=jnp.float32)
        .astype(jnp.bfloat16)
        .reshape(length, HEADS, HEAD_DIM)
    )
    masked_again = attention_scores(queries, key_rows, allowed, score_scale)
    attn_exact = jnp.exp(masked_again - log_total)
    probs_again = attn_exact.astype(jnp.bfloat16)
    grad_values = jnp.einsum(
        "hqk,qhd->khd", probs_again, grad_attended, preferred_element_type=jnp.float32
    )
    grad_probs = jnp.einsum(
        "qhd,khd->hqk", grad_attended, values, preferred_element_type=jnp.float32
    )
    row_dot = jnp.sum(attn_exact * grad_probs, axis=-1, keepdims=True)
    grad_scores = (attn_exact * (grad_probs - row_dot)).astype(jnp.bfloat16)
    grad_queries = (
        jnp.einsum("hqk,khd->qhd", grad_scores, key_rows, preferred_element_type=jnp.float32)
        * score_scale
    )
    grad_keys = (
        jnp.einsum("hqk,qhd->khd", grad_scores, queries, preferred_element_type=jnp.float32)
        * score_scale
    )
    grad_query_unit = rotate(grad_queries, -1.0).reshape(length, D)
    grad_keys_unit = rotate(grad_keys, -1.0).reshape(length, D)
    grad_gain_query = jnp.sum(grad_query_unit * unit_query, axis=0)
    grad_gain_keys = jnp.sum(grad_keys_unit * unit_keys, axis=0)
    grad_query_raw = norm_back(grad_query_unit * gains_back[1], unit_query, inverse_query)
    grad_keys_raw = norm_back(grad_keys_unit * gains_back[2], unit_keys, inverse_keys)
    grad_project = jnp.concatenate(
        [grad_query_raw, grad_keys_raw, grad_values.reshape(length, D)], axis=1
    ).astype(jnp.bfloat16)
    grad_normed = jnp.einsum(
        "sb,ab->sa", grad_project, qkv_back, preferred_element_type=jnp.float32
    )
    grad_gain_first = jnp.sum(grad_normed * unit_first, axis=0)
    grad_inputs = grad_middle + norm_back(grad_normed * gains_back[0], unit_first, inverse_first)
    grad_gains = jnp.stack(
        [grad_gain_first, grad_gain_query, grad_gain_keys, grad_gain_ffn], axis=0
    )
    grad_qkv = jnp.einsum("sa,sb->ab", normed, grad_project, preferred_element_type=jnp.float32)
    grad_attn_out = jnp.einsum(
        "sa,sb->ab", attended, grad_branch, preferred_element_type=jnp.float32
    )
    owned_qkv, owned_attn_out, owned_gains = (
        lax.psum_scatter(
            grad_qkv.astype(jnp.bfloat16), "shard", scatter_dimension=0, tiled=True
        ).astype(jnp.float32),
        lax.psum_scatter(
            grad_attn_out.astype(jnp.bfloat16), "shard", scatter_dimension=0, tiled=True
        ).astype(jnp.float32),
        lax.psum_scatter(
            grad_gains.astype(jnp.bfloat16), "shard", scatter_dimension=1, tiled=True
        ).astype(jnp.float32),
    )
    summed_gains, summed_qkv, summed_attn_out, summed_in, summed_out = (
        lax.psum(owned_gains.astype(jnp.bfloat16), "rep").astype(jnp.float32),
        lax.psum(owned_qkv.astype(jnp.bfloat16), "rep").astype(jnp.float32),
        lax.psum(owned_attn_out.astype(jnp.bfloat16), "rep").astype(jnp.float32),
        lax.psum(in_grads.astype(jnp.bfloat16), "rep").astype(jnp.float32),
        lax.psum(out_grads.astype(jnp.bfloat16), "rep").astype(jnp.float32),
    )
    return (
        output,
        grad_inputs.astype(jnp.bfloat16),
        summed_gains,
        summed_qkv,
        summed_attn_out,
        summed_in,
        summed_out,
    )


def solution(mesh):
    placed = (
        P(("rep", "shard"), None),
        P(None, "shard"),
        P("shard", None),
        P("shard", None),
        P(None, "shard", None),
        P(None, "shard", None),
        P(("rep", "shard"), None),
        P(("rep", "shard"), None),
        P(("rep", "shard")),
        P(("rep", "shard"), None),
    )
    return jax.shard_map(
        body,
        mesh=mesh,
        in_specs=placed,
        out_specs=(
            P(("rep", "shard"), None),
            P(("rep", "shard"), None),
            P(None, "shard"),
            P("shard", None),
            P("shard", None),
            P(None, "shard", None),
            P(None, "shard", None),
        ),
        check_vma=False,
    )
```

profile of v0, /device:TPU:0, one launch (start us, length us, event | category | flops | bytes accessed | tf_op | source)
XLA Modules:
  0.0 2282.3 jit_solution(8791907840076502041)
XLA Ops:
  26.2 6.7 gather_fusion.2
  37.2 86.3 %all_to_all.138 = bf16[16,72,2048]{2,1,0:T(8,128)(2,1)} all-to-all(bf16[16,72,2048]{2,1,0:T(8,128)(2,1)S(1)} %multiply_convert_fusion), channel_id=1, replica_groups=mesh['rep'=4,'shard'=8] {'shard'}, dimensions={0} | all-to-all | bytes 9437184 | tf_op jit(solution)/shard_map/all_to_all | solution.py:166
  123.4 5.0 all-to-all-start.2
  129.2 139.0 %all-to-all-done.2 = bf16[16,256,1024]{2,1,0:T(8,128)(2,1)} async-done(((bf16[16,256,1024]{2,1,0:T(8,128)(2,1)}), bf16[16,256,1024]{2,1,0:T(8,128)(2,1)}, u32[]{:S(2)}, u32[]{:S(2)}) %all-to-all-start.2) | async-done | bytes 8388640 | tf_op jit(solution)/shard_map/all_to_all | solution.py:150
  268.2 5.8 all-to-all-start.1
  279.1 215.5 %all_gather.12 = bf16[4,2048]{1,0:T(4,128)(2,1)S(1)} all-gather(bf16[4,256]{1,0:T(4,128)(2,1)S(1)} %copy-done.48), channel_id=1, replica_groups=mesh['rep'=4,'shard'=8] {'shard'}, dimensions={1}, use_global_device_ids=true | all-gather | bytes 18432 | tf_op jit(solution)/shard_map/all_gather | solution.py:112
  495.9 10.1 fusion.30
  512.0 4.9 multiply_reduce_fusion.5
  518.1 5.9 gather_fusion
  524.0 4.9 broadcast_select_fusion
  528.9 4.8 all-to-all-start
  533.8 5.2 copy.97
  539.0 7.9 copy.92
  547.0 14.2 copy.91
  561.1 27.4 %all-to-all-done = bf16[16,72,2048]{2,1,0:T(8,128)(2,1)} async-done(((bf16[16,72,2048]{2,1,0:T(8,128)(2,1)}), bf16[16,72,2048]{2,1,0:T(8,128)(2,1)}, u32[]{:S(2)}, u32[]{:S(2)}) %all-to-all-start) | async-done | bytes 4718624 | tf_op jit(solution)/shard_map/all_to_all | solution.py:152
  591.4 18.2 fusion.60
  609.7 10.4 multiply_convert_fusion.2
  621.5 7.2 convolution_convert_fusion.5
  628.6 9.4 copy.93
  642.6 15.9 convolution_convert_fusion.4
  658.5 9.4 copy.98
  667.9 29.5 %all-to-all-done.3 = bf16[2,576,2048]{2,0,1:T(2,128)(2,1)} async-done(((bf16[2,576,2048]{2,0,1:T(2,128)(2,1)}), bf16[2,576,2048]{2,0,1:T(2,128)(2,1)}, u32[]{:S(2)}, u32[]{:S(2)}) %all-to-all-start.3) | async-done | bytes 4718624 | tf_op jit(solution)/shard_map/all_to_all | solution.py:154
  697.4 4.6 all-to-all-start.5
  702.2 6.6 copy.94
  708.9 11.8 gather_fusion.1
  720.7 6.5 fusion
  727.1 29.6 %all-to-all-done.5 = bf16[2,576,2048]{2,0,1:T(2,128)(2,1)} async-done(((bf16[2,576,2048]{2,0,1:T(2,128)(2,1)}), bf16[2,576,2048]{2,0,1:T(2,128)(2,1)}, u32[]{:S(2)}, u32[]{:S(2)}) %all-to-all-start.5) | async-done | bytes 4718624 | tf_op jit(solution)/shard_map/all_to_all | solution.py:170
  756.7 6.6 copy.99
  763.4 11.9 gather_fusion.3
  775.4 5.2 convert_reduce_fusion
  783.1 5.6 convolution_convert_fusion.2
  788.8 7.5 convolution_convert_fusion.6
  812.1 14.8 convolution_convert_fusion
  828.6 9.3 convolution_convert_fusion.3
  838.0 29.2 %copy.115 = bf16[2,2048,1024]{2,0,1:T(2,128)(2,1)} copy(bf16[2,2048,1024]{2,1,0:T(8,128)(2,1)S(1)} %convolution_convert_fusion.3) | data formatting | bytes 16777216 | tf_op jit(solution)/shard_map/convert_element_type | solution.py:176
  867.2 5.4 all-to-all-start.7
  872.6 22.1 convolution_convert_fusion.1
  894.7 31.1 %copy.113 = bf16[2,2048,2048]{2,0,1:T(2,128)(2,1)} copy(bf16[2,2048,2048]{2,1,0:T(8,128)(2,1)} %convolution_convert_fusion.1) | data formatting | bytes 33554432 | tf_op jit(solution)/shard_map/convert_element_type | solution.py:173
  925.8 97.7 %all-to-all-done.7 = bf16[2,2048,1024]{2,0,1:T(2,128)(2,1)} async-done(((bf16[2,2048,1024]{2,0,1:T(2,128)(2,1)}), bf16[2,2048,1024]{2,0,1:T(2,128)(2,1)}, u32[]{:S(2)}, u32[]{:S(2)}) %all-to-all-start.7) | async-done | bytes 8388640 | tf_op jit(solution)/shard_map/all_to_all | solution.py:175
  1023.5 5.9 all-to-all-start.6
  1029.5 13.5 fusion.15
  1044.5 9.4 copy.116
  1053.8 195.8 %all-to-all-done.6 = bf16[2,2048,2048]{2,0,1:T(2,128)(2,1)} async-done(((bf16[2,2048,2048]{2,0,1:T(2,128)(2,1)}), bf16[2,2048,2048]{2,0,1:T(2,128)(2,1)}, u32[]{:S(2)}, u32[]{:S(2)}) %all-to-all-start.6) | async-done | bytes 16777248 | tf_op jit(solution)/shard_map/all_to_all | solution.py:172
  1249.7 17.3 copy.114
  1270.3 12.1 psum.35
  1283.0 955.3 %all-reduce.3.cloned.1.call-done = (bf16[256,6144]{1,0:T(8,128)(2,1)}, bf16[256,2048]{1,0:T(8,128)(2,1)}, bf16[16,256,2048]{2,1,0:T(8,128)(2,1)}, bf16[16,256,1024]{2,1,0:T(8,128)(2,1)}) async-done(((bf16[256,6144]{1,0:T(8,128)(2,1)}, bf16[256,2048]{1,0:T(8,128)(2,1)}, bf16[16,256,2048]{2,1,0:T(8,128)(2,1)}, bf16[16,256,1024]{2,1,0:T(8,128)(2,1)}), (bf16[256,6144]{1,0:T(8,128)(2,1)}, ...) | async-done | bytes 29360144 | tf_op jit(solution)/shard_map/psum | solution.py:251
  2244.7 11.7 convert_element_type.159
  2256.4 18.8 convert_element_type.157
  (214 shorter events, 77.4 us)
Async XLA Ops:
  7.2 488.7 %all-gather.3.cloned.1.call-start = ((), (), s32[]{:S(2)}) async-start(), calls=%async_computation.11 | async-start | bytes 28311552 | tf_op jit(solution)/shard_map/all_gather | solution.py:113
  123.4 144.7 %all-to-all-start.2 = ((bf16[16,256,1024]{2,1,0:T(8,128)(2,1)}), bf16[16,256,1024]{2,1,0:T(8,128)(2,1)}, u32[]{:S(2)}, u32[]{:S(2)}) async-start(bf16[16,256,1024]{2,1,0:T(8,128)(2,1)} %param.15), calls=%async_computation.2 | async-start | bytes 16777216 | tf_op jit(solution)/shard_map/all_to_all | solution.py:150
  128.4 383.6 %all-gather.5.cloned.1.call-start = ((), (), s32[]{:S(2)}) async-start(), calls=%async_computation.12 | async-start | bytes 9437184 | tf_op jit(solution)/shard_map/all_gather | solution.py:114
  129.2 149.9 %copy-start.48 = (bf16[4,256]{1,0:T(4,128)(2,1)S(1)}, bf16[4,256]{1,0:T(4,128)(2,1)}, u32[]{:S(2)}) copy-start(bf16[4,256]{1,0:T(4,128)(2,1)} %param.11) | copy-start | bytes 6148
  129.2 365.4 %copy-start.7 = (bf16[128,2048]{1,0:T(8,128)(2,1)S(1)}, bf16[128,2048]{1,0:T(8,128)(2,1)}, u32[]{:S(2)}) copy-start(bf16[128,2048]{1,0:T(8,128)(2,1)} %param.10) | copy-start | bytes 1572868
  268.2 260.8 %all-to-all-start.1 = ((bf16[16,256,2048]{2,1,0:T(8,128)(2,1)}), bf16[16,256,2048]{2,1,0:T(8,128)(2,1)}, u32[]{:S(2)}, u32[]{:S(2)}) async-start(bf16[16,256,2048]{2,1,0:T(8,128)(2,1)} %param.14), calls=%async_computation.1 | async-start | bytes 33554432 | tf_op jit(solution)/shard_map/all_to_all | solution.py:149
  494.8 11.2 copy-start.40
  495.8 12.1 copy-start.25
  495.8 10.2 copy-start.29
  495.8 10.5 copy-start.36
  495.8 10.5 copy-start.38
  495.8 21.2 copy-start.34
  506.0 4.2 copy-start
  512.0 5.0 copy-start.9
  517.0 7.0 copy-start.46
  528.9 59.6 %all-to-all-start = ((bf16[16,72,2048]{2,1,0:T(8,128)(2,1)}), bf16[16,72,2048]{2,1,0:T(8,128)(2,1)}, u32[]{:S(2)}, u32[]{:S(2)}) async-start(bf16[16,72,2048]{2,1,0:T(8,128)(2,1)} %broadcast_select_fusion), calls=%async_computation | async-start | bytes 9437184 | tf_op jit(solution)/shard_map/all_to_all | solution.py:152
  588.5 21.1 slice-start
  588.5 21.1 slice-start.2
  591.4 18.2 copy-start.19
  591.4 18.2 slice-start.1
  591.4 18.2 slice-start.3
  620.1 22.6 copy-start.51
  638.0 59.3 %all-to-all-start.3 = ((bf16[2,576,2048]{2,0,1:T(2,128)(2,1)}), bf16[2,576,2048]{2,0,1:T(2,128)(2,1)}, u32[]{:S(2)}, u32[]{:S(2)}) async-start(bf16[2,576,2048]{2,0,1:T(2,128)(2,1)} %copy.93), calls=%async_computation.3 | async-start | bytes 9437184 | tf_op jit(solution)/shard_map/all_to_all | solution.py:154
  697.4 59.4 %all-to-all-start.5 = ((bf16[2,576,2048]{2,0,1:T(2,128)(2,1)}), bf16[2,576,2048]{2,0,1:T(2,128)(2,1)}, u32[]{:S(2)}, u32[]{:S(2)}) async-start(bf16[2,576,2048]{2,0,1:T(2,128)(2,1)} %copy.98), calls=%async_computation.5 | async-start | bytes 9437184 | tf_op jit(solution)/shard_map/all_to_all | solution.py:170
  702.0 565.0 %reduce-scatter.8.cloned.1.call-start = ((), (), s32[]{:S(2)}) async-start(), calls=%async_computation.14 | async-start | bytes 9437184 | tf_op jit(solution)/shard_map/reduce_scatter | solution.py:242
  708.9 11.8 copy-start.28
  775.3 5.2 copy-start.6
  775.3 5.2 copy-start.35
  775.3 5.2 copy-start.47
  775.4 5.6 copy-start.24
  788.7 9.8 copy-start.33
  788.7 14.9 copy-start.1
  788.7 478.3 %reduce-scatter.6.cloned.1.call-start = ((), (), s32[]{:S(2)}) async-start(), calls=%async_computation.13 | async-start | bytes 28311552 | tf_op jit(solution)/shard_map/reduce_scatter | solution.py:239
  803.6 3.5 copy-start.16
  803.6 3.5 copy-start.18
  803.6 4.0 copy-start.12
  803.6 4.0 copy-start.14
  805.6 2.6 copy-start.26
  867.2 5.4 copy-start.52
  867.2 156.3 %all-to-all-start.7 = ((bf16[2,2048,1024]{2,0,1:T(2,128)(2,1)}), bf16[2,2048,1024]{2,0,1:T(2,128)(2,1)}, u32[]{:S(2)}, u32[]{:S(2)}) async-start(bf16[2,2048,1024]{2,0,1:T(2,128)(2,1)} %copy.115), calls=%async_computation.9 | async-start | bytes 16777216 | tf_op jit(solution)/shard_map/all_to_all | solution.py:175
  925.8 103.7 %copy-start.8 = (bf16[128,2048]{1,0:T(8,128)(2,1)S(1)}, bf16[128,2048]{1,0:T(8,128)(2,1)}, u32[]{:S(2)}) copy-start(bf16[128,2048]{1,0:T(8,128)(2,1)} %param.10) | copy-start | bytes 1572868
  925.8 103.7 %copy-start.21 = (bf16[128,2048]{1,0:T(8,128)(2,1)S(1)}, bf16[128,2048]{1,0:T(8,128)(2,1)}, u32[]{:S(2)}) copy-start(bf16[128,2048]{1,0:T(8,128)(2,1)} %copy.125) | copy-start | bytes 1572868
  925.8 103.7 %copy-start.22 = (bf16[128,2048]{1,0:T(8,128)(2,1)S(1)}, bf16[128,2048]{1,0:T(8,128)(2,1)}, u32[]{:S(2)}) copy-start(bf16[128,2048]{1,0:T(8,128)(2,1)} %get-tuple-element.26) | copy-start | bytes 1572868
  925.8 103.7 %copy-start.23 = (bf16[128,2048]{1,0:T(8,128)(2,1)S(1)}, bf16[128,2048]{1,0:T(8,128)(2,1)}, u32[]{:S(2)}) copy-start(bf16[128,2048]{1,0:T(8,128)(2,1)} %get-tuple-element.27) | copy-start | bytes 1572868
  1023.5 226.2 %all-to-all-start.6 = ((bf16[2,2048,2048]{2,0,1:T(2,128)(2,1)}), bf16[2,2048,2048]{2,0,1:T(2,128)(2,1)}, u32[]{:S(2)}, u32[]{:S(2)}) async-start(bf16[2,2048,2048]{2,0,1:T(2,128)(2,1)} %copy.113), calls=%async_computation.8 | async-start | bytes 33554432 | tf_op jit(solution)/shard_map/all_to_all | solution.py:172
  1029.4 240.0 %reduce-scatter.10.cloned.1.call-start = ((), (), s32[]{:S(2)}) async-start(), calls=%async_computation.15 | async-start | bytes 589824
  1044.2 1194.1 %all-reduce.3.cloned.1.call-start = ((), (), s32[]{:S(2)}) async-start(), calls=%async_computation.16 | async-start | bytes 58720256 | tf_op jit(solution)/shard_map/psum | solution.py:251
  2238.3 2.9 copy-start.20
  (22 other events, 28.5 us)
Sparse Core Ops, SparseCore 0:
  9.9 238.3 all-gather.2
  250.2 176.0 all-gather.4
  788.8 70.3 reduce-scatter.7
  863.7 329.4 reduce-scatter.5
  1197.0 35.8 reduce-scatter.9
  1267.2 971.1 all-reduce.2
where the time goes:
time: 2290 us; the launch traced here: 2280 us
  waiting for transfers between devices  1480 us (65%)
  blocking collectives  314 us (14%)
  local copies, waits for them, and re-layouts  217 us (9%)
  matrix products  147 us (6%)
  other arithmetic  76.3 us (3%)
  starting transfers between devices  36.7 us (2%)
    psum x1, waiting for transfers between devices, body(): lax.psum(owned_qkv.astype(jnp.bfloat16), 'rep').astype(jnp.float32)  955 us
    all_gather x1, blocking collectives, body(): lax.all_gather(norm_gains, 'shard', axis=1, tiled=True)  216 us
    all_to_all x1, waiting for transfers between devices, body(): lax.all_to_all(grad_in.astype(jnp.bfloat16), 'shard', split_axis=1, conca...  196 us
    all_to_all x1, waiting for transfers between devices, body(): lax.all_to_all(w_out, 'shard', split_axis=0, concat_axis=1, tiled=True)  139 us
    all_to_all x1, waiting for transfers between devices, body(): lax.all_to_all(grad_out.astype(jnp.bfloat16), 'shard', split_axis=1, conc...  97.7 us
    all_to_all x1, blocking collectives, body(): lax.all_to_all(grad_slots, 'shard', split_axis=0, concat_axis=1, tiled=True)  86.3 us
  transfers between devices with their start and end apart: 13, of which 7 were waited for; matrix products, arithmetic and copies ran while one was open for 14% of the time, Pallas kernels for 0%

commit v1 on v0

v1 whole, which is shorter than its diff:
```python
import math

import jax
import jax.numpy as jnp
from jax import lax
from jax.sharding import PartitionSpec as P

D = 2048
HEADS = 16
HEAD_DIM = 128
FF = 1024
EXPERTS = 16
TOPK = 8
CAP = 72

epsilon = 1e-05
masked_value = -1e30
bf16 = jnp.bfloat16
f32 = jnp.float32


def swap(array, axis, distance):
    count = lax.axis_size(axis)
    return lax.ppermute(array, axis, [(i, i ^ distance) for i in range(count)])


def gather_chips(block):
    chips = lax.axis_size("shard") // 2
    return jnp.stack([block] + [swap(block, "shard", 2 * m) for m in range(1, chips)])


def join_cores(blocks):
    return jnp.stack([blocks, swap(blocks, "shard", 1)])


def gather_group(block):
    return join_cores(gather_chips(block)).reshape((-1,) + block.shape)


def gather_everywhere(block):
    reps = lax.axis_size("rep")
    mine = gather_chips(block)
    far = jnp.stack([swap(mine, "rep", r) for r in range(1, reps)])
    near = join_cores(mine).reshape((-1,) + block.shape)
    far_both = jnp.stack([far, swap(far, "shard", 1)], axis=1)
    return near, far_both.reshape((-1,) + block.shape)


def scatter_group(partial):
    count = partial.shape[0]
    half = count // 2
    partial = partial.astype(bf16)
    chip_sum = partial[:half].astype(f32) + swap(partial[half:], "shard", 1).astype(f32)
    total = chip_sum[0]
    sent = chip_sum.astype(bf16)
    for m in range(1, half):
        total = total + swap(sent[m], "shard", 2 * m).astype(f32)
    return total


def sum_group(small):
    kinds, count, length = small.shape
    bits = count.bit_length() - 1
    small = small.reshape((kinds,) + (2,) * bits + (length,))
    for bit in range(bits):
        axis = 1 if bit == 0 else 1 + bits - bit
        small = small + jnp.flip(swap(small, "shard", 1 << bit), axis)
    return small.reshape(kinds, count, length)


def exchange(array):
    return lax.all_to_all(array, "shard", split_axis=0, concat_axis=0, tiled=True)


def norm_parts(vector):
    inverse = lax.rsqrt(jnp.mean(vector * vector, axis=-1, keepdims=True) + epsilon)
    return (vector * inverse, inverse)


def norm_back(upstream, unit_rows, inverse):
    return inverse * (upstream - unit_rows * jnp.mean(upstream * unit_rows, axis=-1, keepdims=True))


def rope_tables(length):
    halfway = HEAD_DIM // 2
    frequency = 10000.0 ** (-jnp.arange(halfway, dtype=f32) / halfway)
    angles = jnp.arange(length, dtype=f32)[:, None] * frequency[None, :]
    return jnp.cos(angles), jnp.sin(angles)


def rotate(vector, cosine, sine):
    halfway = HEAD_DIM // 2
    first_half = vector[..., :halfway]
    second_half = vector[..., halfway:]
    return jnp.concatenate(
        [first_half * cosine - second_half * sine, second_half * cosine + first_half * sine],
        axis=-1,
    )


def dot(a, b, contract):
    return lax.dot_general(a, b, ((contract[0], contract[1]), ((), ())), preferred_element_type=f32)


def body(
    tokens, norm_gains, w_qkv, w_attn_out, w_in, w_out, route_gates, routes, prefix, cotangent
):
    length = tokens.shape[0]
    group = lax.axis_size("shard")
    reps = lax.axis_size("rep")
    local_experts = EXPERTS // group
    local_heads = HEADS // group
    width = D // group
    rank = lax.axis_index("shard")
    score_scale = 1.0 / math.sqrt(HEAD_DIM)

    qkv_cols = exchange(
        w_qkv.reshape(width, 3, group, width).transpose(2, 0, 1, 3)
    ).reshape(D, 3 * width)
    gains_full = (
        exchange(jnp.broadcast_to(norm_gains[None], (group,) + norm_gains.shape))
        .transpose(1, 0, 2)
        .reshape(4, D)
        .astype(f32)
    )
    weights_in, weights_out = [], []
    for j in range(local_experts):
        rows = slice(j * group, (j + 1) * group)
        weights_in.append(exchange(w_in[rows]).reshape(D, 2 * FF))
        weights_out.append(exchange(w_out[rows]).reshape(D, FF))

    named = routes[:, :, None] == jnp.arange(EXPERTS, dtype=jnp.int32)[None, None, :]
    member = jnp.any(named, axis=1)
    gate_of = jnp.sum(jnp.where(named, route_gates[:, :, None], 0.0), axis=1)
    earlier = (jnp.arange(length)[:, None] > jnp.arange(length)[None, :]).astype(f32)
    place = jnp.dot(earlier, member.astype(f32))
    place = jnp.where(member, place, -1.0)
    tables = jnp.stack([place.T, gate_of.T])

    tokens_near = gather_group(tokens).reshape(group * length, D)
    prefix_near = gather_group(jnp.broadcast_to(prefix[:, None], (8, 128)))[:, 0, 0]
    tables_near, tables_far = gather_everywhere(tables)
    dy_near, dy_far = gather_everywhere(cotangent)

    unit_first, inverse_first = norm_parts(tokens_near.astype(f32))
    normed = (unit_first * gains_full[0]).astype(bf16)
    project = jnp.dot(normed, qkv_cols, preferred_element_type=f32)
    q_raw, k_raw = project[:, :width], project[:, width : 2 * width]
    squares = jnp.stack([jnp.sum(q_raw * q_raw, axis=-1), jnp.sum(k_raw * k_raw, axis=-1)])
    inverse_qk = lax.rsqrt(
        sum_group(squares.reshape(2, group, length)).reshape(2, -1) / D + epsilon
    )
    inverse_query, inverse_keys = inverse_qk[0][:, None], inverse_qk[1][:, None]
    unit_query, unit_keys = q_raw * inverse_query, k_raw * inverse_keys
    own_gains = norm_gains.astype(f32)
    cosine, sine = rope_tables(length)

    def heads_of(array):
        return array.reshape(group, length, local_heads, HEAD_DIM).transpose(0, 2, 1, 3)

    def rows_of(array):
        return array.transpose(0, 2, 1, 3).reshape(group * length, width)

    queries = rotate(heads_of(unit_query * own_gains[1]), cosine, sine).astype(bf16)
    key_rows = rotate(heads_of(unit_keys * own_gains[2]), cosine, sine).astype(bf16)
    values = heads_of(project[:, 2 * width :].astype(bf16))
    positions = jnp.arange(length, dtype=jnp.int32)
    allowed = (positions[None, None, :] <= positions[None, :, None]) | (
        positions[None, None, :] < prefix_near[:, None, None]
    )
    scores = jnp.einsum("nhqd,nhkd->nhqk", queries, key_rows, preferred_element_type=f32)
    masked = jnp.where(allowed[:, None], scores * score_scale, masked_value)
    top_score = jnp.max(masked, axis=-1, keepdims=True)
    powers = jnp.exp(masked - top_score)
    attn_exact = powers / jnp.sum(powers, axis=-1, keepdims=True)
    attn_probs = attn_exact.astype(bf16)
    attended = rows_of(
        jnp.einsum("nhqk,nhkd->nhqd", attn_probs, values, preferred_element_type=f32)
    ).astype(bf16)
    branch_part = jnp.dot(attended, w_attn_out, preferred_element_type=f32)
    branch = scatter_group(branch_part.reshape(group, length, D))
    middle = tokens.astype(f32) + branch
    unit_second, inverse_second = norm_parts(middle)
    normed_ffn = (unit_second * gains_full[3]).astype(bf16)
    ffn_near, ffn_far = gather_everywhere(normed_ffn)

    ffn_all = jnp.concatenate([ffn_near, ffn_far])
    dy_all = jnp.concatenate([dy_near, dy_far])
    tables_all = jnp.concatenate([tables_near, tables_far])
    near = group * CAP
    mix_part = 0.0
    grad_ffn_part = 0.0
    sent_in, sent_out = [], []
    for j in range(local_experts):
        expert = j * group + rank
        mine = lax.dynamic_index_in_dim(tables_all, expert, axis=2, keepdims=False)
        place_of, gates_of = mine[:, 0], mine[:, 1]
        hit = place_of[:, None, :] == jnp.arange(CAP, dtype=f32)[None, :, None]
        pick = hit.astype(bf16)
        weighted = jnp.where(hit, gates_of[:, None, :], 0.0).astype(bf16)
        slot_rows = (
            jnp.einsum("nst,ntd->nsd", pick, ffn_all, preferred_element_type=f32)
            .astype(bf16)
            .reshape(-1, D)
        )
        slot_grads = (
            jnp.einsum("nst,ntd->nsd", weighted, dy_all, preferred_element_type=f32)
            .astype(bf16)
            .reshape(-1, D)
        )
        gate_up = jnp.dot(slot_rows, weights_in[j], preferred_element_type=f32)
        gate, up = gate_up[:, :FF], gate_up[:, FF:]
        sigmoid_gate = jax.nn.sigmoid(gate)
        silu_gate = gate * sigmoid_gate
        hidden = (silu_gate * up).astype(bf16)
        grad_hidden = jnp.dot(slot_grads, weights_out[j], preferred_element_type=f32)
        grad_gate = grad_hidden * up * sigmoid_gate * (1.0 + gate * (1.0 - sigmoid_gate))
        grad_up = grad_hidden * silu_gate
        grad_gate_up = jnp.concatenate([grad_gate, grad_up], axis=-1).astype(bf16)
        out_rows = dot(hidden[:near], weights_out[j], ((1,), (1,))).astype(bf16)
        mix_part = mix_part + jnp.einsum(
            "nst,nsd->ntd",
            weighted[:group],
            out_rows.reshape(group, CAP, D),
            preferred_element_type=f32,
        )
        grad_rows = dot(grad_gate_up[:near], weights_in[j], ((1,), (1,))).astype(bf16)
        grad_ffn_part = grad_ffn_part + jnp.einsum(
            "nst,nsd->ntd",
            pick[:group],
            grad_rows.reshape(group, CAP, D),
            preferred_element_type=f32,
        )
        grad_out = dot(slot_grads, hidden, ((0,), (0,))).astype(bf16)
        grad_in = dot(slot_rows, grad_gate_up, ((0,), (0,))).astype(bf16)
        sent_out.append(exchange(grad_out.reshape(group, width, FF)))
        sent_in.append(exchange(grad_in.reshape(group, width, 2 * FF)))
    in_grad = jnp.concatenate(sent_in).astype(f32)
    out_grad = jnp.concatenate(sent_out).astype(f32)
    output = (middle + scatter_group(mix_part)).astype(bf16)

    grad_normed_ffn = scatter_group(grad_ffn_part)
    grad_gain_ffn = jnp.sum(grad_normed_ffn * unit_second, axis=0)
    grad_middle = cotangent.astype(f32) + norm_back(
        grad_normed_ffn * gains_full[3], unit_second, inverse_second
    )
    grad_branch = gather_group(grad_middle.astype(bf16)).reshape(group * length, D)
    grad_attended = heads_of(dot(grad_branch, w_attn_out, ((1,), (1,))).astype(bf16))
    grad_attn_out = dot(attended, grad_branch, ((0,), (0,)))
    grad_values = jnp.einsum(
        "nhqk,nhqd->nhkd", attn_probs, grad_attended, preferred_element_type=f32
    )
    grad_probs = jnp.einsum("nhqd,nhkd->nhqk", grad_attended, values, preferred_element_type=f32)
    row_dot = jnp.sum(attn_exact * grad_probs, axis=-1, keepdims=True)
    grad_scores = (attn_exact * (grad_probs - row_dot)).astype(bf16)
    grad_queries = (
        jnp.einsum("nhqk,nhkd->nhqd", grad_scores, key_rows, preferred_element_type=f32)
        * score_scale
    )
    grad_keys = (
        jnp.einsum("nhqk,nhqd->nhkd", grad_scores, queries, preferred_element_type=f32)
        * score_scale
    )
    grad_query_unit = rows_of(rotate(grad_queries, cosine, -sine))
    grad_keys_unit = rows_of(rotate(grad_keys, cosine, -sine))
    grad_gain_query = jnp.sum(grad_query_unit * unit_query, axis=0)
    grad_gain_keys = jnp.sum(grad_keys_unit * unit_keys, axis=0)
    grad_query_unit = grad_query_unit * own_gains[1]
    grad_keys_unit = grad_keys_unit * own_gains[2]
    means = sum_group(
        jnp.stack(
            [
                jnp.sum(grad_query_unit * unit_query, axis=-1),
                jnp.sum(grad_keys_unit * unit_keys, axis=-1),
            ]
        ).reshape(2, group, length)
    ).reshape(2, -1) / D
    grad_query_raw = inverse_query * (grad_query_unit - unit_query * means[0][:, None])
    grad_keys_raw = inverse_keys * (grad_keys_unit - unit_keys * means[1][:, None])
    grad_project = jnp.concatenate(
        [grad_query_raw, grad_keys_raw, rows_of(grad_values)], axis=1
    ).astype(bf16)
    grad_normed = scatter_group(
        dot(grad_project, qkv_cols, ((1,), (1,))).reshape(group, length, D)
    )
    unit_own, inverse_own = norm_parts(tokens.astype(f32))
    grad_gain_first = jnp.sum(grad_normed * unit_own, axis=0)
    tokens_grad = (
        grad_middle + norm_back(grad_normed * gains_full[0], unit_own, inverse_own)
    ).astype(bf16)

    grad_qkv = dot(normed, grad_project, ((0,), (0,))).astype(bf16)
    slices = grad_qkv.reshape(group, reps, width // reps, 3 * width).transpose(1, 0, 2, 3)
    arrived = lax.all_to_all(
        slices.reshape(reps * group, width // reps, 3 * width),
        ("rep", "shard"),
        split_axis=0,
        concat_axis=0,
        tiled=True,
    ).reshape(reps, group, width // reps, 3, width)
    qkv_slice = (
        jnp.sum(arrived.astype(f32), axis=0)
        .transpose(1, 2, 0, 3)
        .reshape(width // reps, 3 * D)
        .astype(bf16)
    )
    qkv_grad = lax.all_gather(qkv_slice, "rep", axis=0, tiled=True).astype(f32)
    attn_arrived = lax.all_to_all(
        grad_attn_out.astype(bf16), "rep", split_axis=0, concat_axis=0, tiled=True
    ).reshape(reps, width // reps, D)
    attn_slice = jnp.sum(attn_arrived.astype(f32), axis=0).astype(bf16)
    attn_out_grad = lax.all_gather(attn_slice, "rep", axis=0, tiled=True).astype(f32)

    whole = jnp.stack([grad_gain_first, grad_gain_ffn]).reshape(2, group, width).transpose(1, 0, 2)
    owned = jnp.sum(exchange(whole), axis=0)
    gains_grad = lax.psum(
        jnp.stack([owned[0], grad_gain_query, grad_gain_keys, owned[1]]), "rep"
    )
    return (output, tokens_grad, gains_grad, qkv_grad, attn_out_grad, in_grad, out_grad)


def solution(mesh):
    placed = (
        P(("rep", "shard"), None),
        P(None, "shard"),
        P("shard", None),
        P("shard", None),
        P(None, "shard", None),
        P(None, "shard", None),
        P(("rep", "shard"), None),
        P(("rep", "shard"), None),
        P(("rep", "shard")),
        P(("rep", "shard"), None),
    )
    return jax.shard_map(
        body,
        mesh=mesh,
        in_specs=placed,
        out_specs=(
            P(("rep", "shard"), None),
            P(("rep", "shard"), None),
            P(None, "shard"),
            P("shard", None),
            P("shard", None),
            P(None, "shard", None),
            P(None, "shard", None),
        ),
        check_vma=False,
    )
```

time: 2290 us -> 1520 us (0.66)
  waiting for transfers between devices: 1480 us -> 756 us
  blocking collectives: 314 us -> 10.9 us
  starting transfers between devices: 36.7 us -> 214 us
  matrix products: 147 us -> 299 us
  local copies, waits for them, and re-layouts: 217 us -> 80.9 us
  other arithmetic: 76.3 us -> 135 us
    psum x1 -> x0, waiting for transfers between devices: 955 us -> none  [body(): lax.psum(owned_qkv.astype(jnp.bfloat16), 'rep').astype(jnp.float32)]
    ppermute x0 -> x58, waiting for transfers between devices: none -> 647 us  [swap(): return lax.ppermute(array, axis, [(i, i ^ distance) for i in range(count)])]
    all_to_all x7 -> x13, waiting for transfers between devices: 519 us -> 109 us  [the longest x11 67.9 us: exchange(): lax.all_to_all(array, 'shard', split_axis=0, concat_axis=0, tiled=True)]
    all_gather x1 -> x0, blocking collectives: 216 us -> none  [body(): lax.all_gather(norm_gains, 'shard', axis=1, tiled=True)]
    ppermute x0 -> x58, starting transfers between devices: none -> 155 us  [swap(): return lax.ppermute(array, axis, [(i, i ^ distance) for i in range(count)])]
    dot_general x18 -> x32, matrix products: 147 us -> 297 us  [the longest x12 124 us: dot(): lax.dot_general(a, b, ((contract[0], contract[1]), ((), ())), preferred_e...]
    all_to_all x1 -> x0, blocking collectives: 86.3 us -> none  [body(): lax.all_to_all(grad_slots, 'shard', split_axis=0, concat_axis=1, tiled=True)]
    convert_element_type x4 -> x3, local copies, waits for them, and re-layouts: 79.1 us -> 10.6 us  [the longest x1 9.37 us: body(): arrived.astype(f32)]
  transfers between devices with their start and end apart: 13 -> 73, of which waited for: 7 -> 38; matrix products, arithmetic and copies ran while one was open for 14% -> 29% of each run, Pallas kernels for 0% -> 0%
where the time goes in v1:
time: 1520 us; the launch traced here: 1510 us
  waiting for transfers between devices  756 us (50%)
  matrix products  299 us (20%)
  starting transfers between devices  214 us (14%)
  other arithmetic  135 us (9%)
  local copies, waits for them, and re-layouts  80.9 us (5%)
  between operations  16.8 us (1%)
    ppermute x58, waiting for transfers between devices, swap(): return lax.ppermute(array, axis, [(i, i ^ distance) for i in range(count)])  647 us
    ppermute x58, starting transfers between devices, swap(): return lax.ppermute(array, axis, [(i, i ^ distance) for i in range(count)])  155 us
    dot_general x12, matrix products, dot(): lax.dot_general(a, b, ((contract[0], contract[1]), ((), ())), preferred_e...  124 us
    all_to_all x11, waiting for transfers between devices, exchange(): lax.all_to_all(array, 'shard', split_axis=0, concat_axis=0, tiled=True)  67.9 us
    dot_general x2, matrix products, body(): gate_up = jnp.dot(slot_rows, weights_in[j], preferred_element_type=f32)  52.9 us
    all_to_all x11, starting transfers between devices, exchange(): lax.all_to_all(array, 'shard', split_axis=0, concat_axis=0, tiled=True)  50.4 us
    dot_general x2, matrix products, body(): jnp.dot(slot_grads, weights_out[j], preferred_element_type=f32)  48.7 us
    all_to_all x1, waiting for transfers between devices, body(): lax.all_to_all(slices.reshape(reps * group, width // reps, 3 * width), ('...  40.9 us
  transfers between devices with their start and end apart: 73, of which 38 were waited for; matrix products, arithmetic and copies ran while one was open for 29% of the time, Pallas kernels for 0%

profile of v1, /device:TPU:0, one launch (start us, length us, event | category | flops | bytes accessed | tf_op | source)
XLA Modules:
  0.0 1512.6 jit_solution(2650638561229563514)
XLA Ops:
  11.7 11.4 collective-permute-done.4
  23.2 11.7 collective-permute-done.6
  61.1 32.8 %collective-permute-done.2 = s32[8,128]{1,0:T(8,128)S(1)} collective-permute-done((s32[8,128]{1,0:T(8,128)S(1)}, s32[8,128]{1,0:T(8,128)S(1)}, u32[]{:S(2)}, u32[]{:S(2)}) %collective-permute-start.2) | collective-permute-done | bytes 4128 | tf_op jit(solution)/shard_map/ppermute | solution.py:24
  129.9 6.0 convolution_convert_fusion.11
  147.6 5.9 collective-permute-done.35
  153.5 11.9 collective-permute-done.37
  187.6 11.2 collective-permute-done.13
  202.1 11.8 collective-permute-start.23
  213.9 93.6 %collective-permute-done.40 = bf16[4,128,2048]{2,1,0:T(8,128)(2,1)} collective-permute-done((bf16[4,128,2048]{2,1,0:T(8,128)(2,1)}, bf16[4,128,2048]{2,1,0:T(8,128)(2,1)}, u32[]{:S(2)}, u32[]{:S(2)}) %collective-permute-start.40) | collective-permute-done | bytes 2097184 | tf_op jit(solution)/shard_map/ppermute | solution.py:24
  308.3 9.6 fusion.147
  319.8 45.5 %collective-permute-start.28 = (bf16[4,128,2048]{2,1,0:T(8,128)(2,1)S(1)}, bf16[4,128,2048]{2,1,0:T(8,128)(2,1)S(1)}, u32[]{:S(2)}, u32[]{:S(2)}) collective-permute-start(bf16[4,128,2048]{2,1,0:T(8,128)(2,1)S(1)} %get-tuple-element.63), channel_id=1, source_target_pairs={{0,16},{8,24},{16,0},{24,8},{1,17},{9,25},{17,1},{25,9},{2,18},{10... | collective-permute-start | bytes 6291464 | tf_op jit(solution)/shard_map/ppermute | solution.py:24
  367.9 89.3 %collective-permute-done.28 = bf16[4,128,2048]{2,1,0:T(8,128)(2,1)S(1)} collective-permute-done((bf16[4,128,2048]{2,1,0:T(8,128)(2,1)S(1)}, bf16[4,128,2048]{2,1,0:T(8,128)(2,1)S(1)}, u32[]{:S(2)}, u32[]{:S(2)}) %collective-permute-start.28) | collective-permute-done | bytes 2097184 | tf_op jit(solution)/shard_map/ppermute | solution.py:24
  457.8 44.9 %collective-permute-done.27 = bf16[4,128,2048]{2,1,0:T(8,128)(2,1)S(1)} collective-permute-done((bf16[4,128,2048]{2,1,0:T(8,128)(2,1)S(1)}, bf16[4,128,2048]{2,1,0:T(8,128)(2,1)S(1)}, u32[]{:S(2)}, u32[]{:S(2)}) %collective-permute-start.27) | collective-permute-done | bytes 2097184 | tf_op jit(solution)/shard_map/ppermute | solution.py:24
  508.6 6.4 fusion.151
  522.9 91.4 %collective-permute-done.17 = f32[2,16,128]{2,1,0:T(8,128)S(1)} collective-permute-done((f32[2,16,128]{2,1,0:T(8,128)S(1)}, f32[2,16,128]{2,1,0:T(8,128)S(1)}, u32[]{:S(2)}, u32[]{:S(2)}) %collective-permute-start.17) | collective-permute-done | bytes 16416 | tf_op jit(solution)/shard_map/ppermute | solution.py:24
  614.3 42.9 %collective-permute-start.20 = (f32[4,2,16,128]{3,2,1,0:T(8,128)S(1)}, f32[4,2,16,128]{3,2,1,0:T(8,128)S(1)}, u32[]{:S(2)}, u32[]{:S(2)}) collective-permute-start(f32[4,2,16,128]{3,2,1,0:T(8,128)S(1)} %get-tuple-element.89), channel_id=1, source_target_pairs={{0,16},{8,24},{16,0},{24,8},{1,17},{9,25},{17,1},{25,9},{2,18},{10... | collective-permute-start | bytes 196616 | tf_op jit(solution)/shard_map/ppermute | solution.py:24
  694.3 9.6 fusion.26
  703.9 9.6 fusion.25
  723.9 8.2 fusion.23
  737.2 26.5 %fusion.160 = f32[2304,2048]{1,0:T(8,128)} fusion(bf16[2304,2048]{1,0:T(8,128)(2,1)} %bitcast.451, bf16[2048,2048]{1,0:T(8,128)(2,1)} %bitcast.69), kind=kOutput, calls=%fused_computation.302 | convolution fusion | flops 19327352832 | bytes 36700160 | tf_op jit(solution)/shard_map/dot_general | solution.py:211
  763.7 24.4 %multiply_convert_fusion.3 = (bf16[2304,1024]{1,0:T(8,128)(2,1)}, bf16[2304,1024]{1,0:T(8,128)(2,1)}, bf16[2304,1024]{1,0:T(8,128)(2,1)}) fusion(f32[2304,2048]{1,0:T(8,128)} %fusion.160, bf16[2304,2048]{1,0:T(8,128)(2,1)} %bitcast.455, bf16[2048,1024]{1,0:T(8,128)(2,1)} %bitcast.70), kind=kOutput, calls=%fused_computation.21 | convolution fusion | flops 9699065856 | bytes 46661632 | tf_op jit(solution)/shard_map/dot_general | solution.py:216
  788.1 8.2 convolution_convert_fusion.6
  801.0 8.2 fusion.24
  809.2 22.1 %all-to-all-done.4 = bf16[8,256,2048]{2,1,0:T(8,128)(2,1)} async-done(((bf16[8,256,2048]{2,1,0:T(8,128)(2,1)}), bf16[8,256,2048]{2,1,0:T(8,128)(2,1)}, u32[]{:S(2)}, u32[]{:S(2)}) %all-to-all-start.4) | async-done | bytes 8388640 | tf_op jit(solution)/shard_map/all_to_all | solution.py:72
  836.1 26.5 %fusion.161 = f32[2304,2048]{1,0:T(8,128)} fusion(bf16[2304,2048]{1,0:T(8,128)(2,1)} %bitcast.447, bf16[2048,2048]{1,0:T(8,128)(2,1)} %bitcast.76), kind=kOutput, calls=%fused_computation.303 | convolution fusion | flops 19327352832 | bytes 36700160 | tf_op jit(solution)/shard_map/dot_general | solution.py:211
  862.5 22.7 %all-to-all-done.5 = bf16[8,256,1024]{2,1,0:T(8,128)(2,1)} async-done(((bf16[8,256,1024]{2,1,0:T(8,128)(2,1)}), bf16[8,256,1024]{2,1,0:T(8,128)(2,1)}, u32[]{:S(2)}, u32[]{:S(2)}) %all-to-all-start.5) | async-done | bytes 4194336 | tf_op jit(solution)/shard_map/all_to_all | solution.py:72
  885.2 24.3 %multiply_convert_fusion.1 = (bf16[2304,1024]{1,0:T(8,128)(2,1)}, bf16[2304,1024]{1,0:T(8,128)(2,1)}, bf16[2304,1024]{1,0:T(8,128)(2,1)}) fusion(f32[2304,2048]{1,0:T(8,128)} %fusion.161, bf16[2304,2048]{1,0:T(8,128)(2,1)} %bitcast.453, bf16[2048,1024]{1,0:T(8,128)(2,1)} %bitcast.77), kind=kOutput, calls=%fused_computation.19 | convolution fusion | flops 9699065856 | bytes 46661632 | tf_op jit(solution)/shard_map/dot_general | solution.py:216
  909.5 8.8 convolution_convert_fusion.5
  924.8 14.1 convolution_convert_fusion.1
  950.0 15.5 %convolution_convert_fusion = bf16[2048,1024]{1,0:T(8,128)(2,1)} fusion(bf16[2304,2048]{1,0:T(8,128)(2,1)} %bitcast.454, bf16[2304,1024]{1,0:T(8,128)(2,1)} %get-tuple-element.27), kind=kOutput, calls=%fused_computation.52 | convolution fusion | flops 9665773568 | bytes 18350080 | tf_op jit(solution)/shard_map/dot_general | solution.py:102
  965.4 38.1 %collective-permute-done.44 = bf16[128,2048]{1,0:T(8,128)(2,1)S(1)} collective-permute-done((bf16[128,2048]{1,0:T(8,128)(2,1)S(1)}, bf16[128,2048]{1,0:T(8,128)(2,1)S(1)}, u32[]{:S(2)}, u32[]{:S(2)}) %collective-permute-start.44) | collective-permute-done | bytes 524320 | tf_op jit(solution)/shard_map/ppermute | solution.py:24
  1003.5 11.7 collective-permute-done.46
  1026.0 55.7 %collective-permute-done.49 = bf16[128,2048]{1,0:T(8,128)(2,1)S(1)} collective-permute-done((bf16[128,2048]{1,0:T(8,128)(2,1)S(1)}, bf16[128,2048]{1,0:T(8,128)(2,1)S(1)}, u32[]{:S(2)}, u32[]{:S(2)}) %collective-permute-start.49) | collective-permute-done | bytes 524320 | tf_op jit(solution)/shard_map/ppermute | solution.py:24
  1081.8 9.8 collective-permute-done.48
  1105.0 26.5 %fusion.20 = bf16[2048,2048]{1,0:T(8,128)(2,1)} fusion(bf16[2304,2048]{1,0:T(8,128)(2,1)} %bitcast.452, bf16[2304,1024]{1,0:T(8,128)(2,1)} %get-tuple-element.26, bf16[2304,1024]{1,0:T(8,128)(2,1)} %get-tuple-element.25), kind=kOutput, calls=%fused_computation.37 | convolution fusion | flops 19350421504 | bytes 27262976 | tf_op jit(solution)/shard_map/dot_general | solution.py:102
  1158.0 72.7 %collective-permute-done.52 = f32[2,2,2,2,128]{4,3,2,1,0:T(2,128)S(1)} collective-permute-done((f32[2,2,2,2,128]{4,3,2,1,0:T(2,128)S(1)}, f32[2,2,2,2,128]{4,3,2,1,0:T(2,128)S(1)}, u32[]{:S(2)}, u32[]{:S(2)}) %collective-permute-start.52) | collective-permute-done | bytes 8224 | tf_op jit(solution)/shard_map/ppermute | solution.py:24
  1232.3 6.7 convolution_convert_fusion.10
  1255.1 6.7 convolution_convert_fusion.8
  1261.8 23.8 %fusion.17 = bf16[2048,2048]{1,0:T(8,128)(2,1)} fusion(bf16[2304,2048]{1,0:T(8,128)(2,1)S(1)} %bitcast.450, bf16[2304,1024]{1,0:T(8,128)(2,1)} %get-tuple-element.24, bf16[2304,1024]{1,0:T(8,128)(2,1)} %get-tuple-element.23), kind=kOutput, calls=%fused_computation.36 | convolution fusion | flops 19350421504 | bytes 27262976 | tf_op jit(solution)/shard_map/dot_general | solution.py:102
  1285.6 40.9 %all-to-all-done.7 = bf16[32,64,768]{2,1,0:T(8,128)(2,1)} async-done(((bf16[32,64,768]{2,1,0:T(8,128)(2,1)}), bf16[32,64,768]{2,1,0:T(8,128)(2,1)}, u32[]{:S(2)}, u32[]{:S(2)}) %all-to-all-start.7) | async-done | bytes 3145760 | tf_op jit(solution)/shard_map/all_to_all | solution.py:294
  1347.3 5.6 convolution_convert_fusion.3
  1366.2 9.4 convert_element_type.322
  1382.4 10.8 maximum_convert_fusion.1
  1403.1 23.1 %all-to-all-done.10 = bf16[8,256,2048]{2,1,0:T(8,128)(2,1)} async-done(((bf16[8,256,2048]{2,1,0:T(8,128)(2,1)}), bf16[8,256,2048]{2,1,0:T(8,128)(2,1)}, u32[]{:S(2)}, u32[]{:S(2)}) %all-to-all-start.10) | async-done | bytes 8388640 | tf_op jit(solution)/shard_map/all_to_all | solution.py:72
  1426.2 18.2 %maximum_convert_fusion = f32[16,256,2048]{2,1,0:T(8,128)} fusion(bf16[8,256,2048]{2,1,0:T(8,128)(2,1)} %all-to-all-done.10, bf16[8,256,2048]{2,1,0:T(8,128)(2,1)} %all-to-all-done.9), kind=kLoop, calls=%fused_computation.3 | loop fusion | flops 16777216 | bytes 50331648 | tf_op jit(solution)/shard_map/convert_element_type | solution.py:238
  1444.4 14.6 collective-permute-done.55
  1460.5 10.3 collective-permute-done.57
  1486.3 10.9 psum.7
  (455 shorter events, 345.3 us)
Async XLA Ops:
  38.9 56.2 %collective-permute-start.7 = (bf16[4,128,2048]{2,1,0:T(8,128)(2,1)}, bf16[4,128,2048]{2,1,0:T(8,128)(2,1)}, u32[]{:S(2)}, u32[]{:S(2)}) collective-permute-start(bf16[4,128,2048]{2,1,0:T(8,128)(2,1)} %get-tuple-element.68), channel_id=1, source_target_pairs={{0,1},{1,0},{2,3},{3,2},{4,5},{5,4},{6,7},{7,6},{8,9},{9,8},{10,11... | collective-permute-start | bytes 6291464 | tf_op jit(solution)/shard_map/ppermute | solution.py:24
  51.5 49.8 %all-to-all-start.1 = ((bf16[8,256,3,256]{1,3,2,0:T(8,128)(2,1)}), bf16[8,256,3,256]{1,3,2,0:T(8,128)(2,1)}, u32[]{:S(2)}, u32[]{:S(2)}) async-start(bf16[8,256,3,256]{1,3,2,0:T(8,128)(2,1)} %copy.181), calls=%async_computation.1 | async-start | bytes 6291456 | tf_op jit(solution)/shard_map/all_to_all | solution.py:72
  56.6 37.3 %collective-permute-start.2 = (s32[8,128]{1,0:T(8,128)S(1)}, s32[8,128]{1,0:T(8,128)S(1)}, u32[]{:S(2)}, u32[]{:S(2)}) collective-permute-start(s32[8,128]{1,0:T(8,128)S(1)} %broadcast_in_dim.50), channel_id=1, source_target_pairs={{0,6},{1,7},{2,4},{3,5},{4,2},{5,3},{6,0},{7,1},{8,14},{9,15},{10,... | collective-permute-start | bytes 12296 | tf_op jit(solution)/shard_map/ppermute | solution.py:24
  59.5 34.4 %collective-permute-start.1 = (s32[8,128]{1,0:T(8,128)S(1)}, s32[8,128]{1,0:T(8,128)S(1)}, u32[]{:S(2)}, u32[]{:S(2)}) collective-permute-start(s32[8,128]{1,0:T(8,128)S(1)} %broadcast_in_dim.50), channel_id=1, source_target_pairs={{0,4},{1,5},{2,6},{3,7},{4,0},{5,1},{6,2},{7,3},{8,12},{9,13},{10,... | collective-permute-start | bytes 12296 | tf_op jit(solution)/shard_map/ppermute | solution.py:24
  60.0 33.9 %collective-permute-start = (s32[8,128]{1,0:T(8,128)S(1)}, s32[8,128]{1,0:T(8,128)S(1)}, u32[]{:S(2)}, u32[]{:S(2)}) collective-permute-start(s32[8,128]{1,0:T(8,128)S(1)} %broadcast_in_dim.50), channel_id=1, source_target_pairs={{0,2},{1,3},{2,0},{3,1},{4,6},{5,7},{6,4},{7,5},{8,10},{9,11},{10,... | collective-permute-start | bytes 12296 | tf_op jit(solution)/shard_map/ppermute | solution.py:24
  139.3 26.1 %collective-permute-start.37 = (bf16[128,2048]{1,0:T(8,128)(2,1)S(1)}, bf16[128,2048]{1,0:T(8,128)(2,1)S(1)}, u32[]{:S(2)}, u32[]{:S(2)}) collective-permute-start(bf16[128,2048]{1,0:T(8,128)(2,1)S(1)} %copy-done.13), channel_id=1, source_target_pairs={{0,6},{1,7},{2,4},{3,5},{4,2},{5,3},{6,0},{7,1},{8,14},{9,15},{10,... | collective-permute-start | bytes 1572872 | tf_op jit(solution)/shard_map/ppermute | solution.py:24
  147.1 29.0 %collective-permute-start.12 = (bf16[128,2048]{1,0:T(8,128)(2,1)S(1)}, bf16[128,2048]{1,0:T(8,128)(2,1)S(1)}, u32[]{:S(2)}, u32[]{:S(2)}) collective-permute-start(bf16[128,2048]{1,0:T(8,128)(2,1)S(1)} %get-tuple-element.64), channel_id=1, source_target_pairs={{0,2},{1,3},{2,0},{3,1},{4,6},{5,7},{6,4},{7,5},{8,10},{9,11},{10,... | collective-permute-start | bytes 1572872 | tf_op jit(solution)/shard_map/ppermute | solution.py:24
  168.8 138.7 %collective-permute-start.40 = (bf16[4,128,2048]{2,1,0:T(8,128)(2,1)}, bf16[4,128,2048]{2,1,0:T(8,128)(2,1)}, u32[]{:S(2)}, u32[]{:S(2)}) collective-permute-start(bf16[4,128,2048]{2,1,0:T(8,128)(2,1)} %get-tuple-element.58), channel_id=1, source_target_pairs={{0,16},{8,24},{16,0},{24,8},{1,17},{9,25},{17,1},{25,9},{2,18},{10... | collective-permute-start | bytes 6291464 | tf_op jit(solution)/shard_map/ppermute | solution.py:24
  171.4 136.9 %collective-permute-start.39 = (bf16[4,128,2048]{2,1,0:T(8,128)(2,1)}, bf16[4,128,2048]{2,1,0:T(8,128)(2,1)}, u32[]{:S(2)}, u32[]{:S(2)}) collective-permute-start(bf16[4,128,2048]{2,1,0:T(8,128)(2,1)} %get-tuple-element.58), channel_id=1, source_target_pairs={{0,8},{8,0},{16,24},{24,16},{1,9},{9,1},{17,25},{25,17},{2,10},{10... | collective-permute-start | bytes 6291464 | tf_op jit(solution)/shard_map/ppermute | solution.py:24
  172.9 135.4 %collective-permute-start.41 = (bf16[4,128,2048]{2,1,0:T(8,128)(2,1)}, bf16[4,128,2048]{2,1,0:T(8,128)(2,1)}, u32[]{:S(2)}, u32[]{:S(2)}) collective-permute-start(bf16[4,128,2048]{2,1,0:T(8,128)(2,1)} %get-tuple-element.58), channel_id=1, source_target_pairs={{0,24},{8,16},{16,8},{24,0},{1,25},{9,17},{17,9},{25,1},{2,26},{10... | collective-permute-start | bytes 6291464 | tf_op jit(solution)/shard_map/ppermute | solution.py:24
  181.0 334.0 %all-to-all-start.3 = ((bf16[8,256,1024]{2,1,0:T(8,128)(2,1)}), bf16[8,256,1024]{2,1,0:T(8,128)(2,1)}, u32[]{:S(2)}, u32[]{:S(2)}) async-start(bf16[8,256,1024]{2,1,0:T(8,128)(2,1)} %get-tuple-element.32), calls=%async_computation.3 | async-start | bytes 8388608 | tf_op jit(solution)/shard_map/all_to_all | solution.py:72
  201.2 116.9 %collective-permute-start.24 = (bf16[128,2048]{1,0:T(8,128)(2,1)S(1)}, bf16[128,2048]{1,0:T(8,128)(2,1)S(1)}, u32[]{:S(2)}, u32[]{:S(2)}) collective-permute-start(bf16[128,2048]{1,0:T(8,128)(2,1)S(1)} %multiply_convert_fusion.10), channel_id=1, source_target_pairs={{0,4},{1,5},{2,6},{3,7},{4,0},{5,1},{6,2},{7,3},{8,12},{9,13},{10,... | collective-permute-start | bytes 1572872 | tf_op jit(solution)/shard_map/ppermute | solution.py:24
  202.1 116.0 %collective-permute-start.23 = (bf16[128,2048]{1,0:T(8,128)(2,1)S(1)}, bf16[128,2048]{1,0:T(8,128)(2,1)S(1)}, u32[]{:S(2)}, u32[]{:S(2)}) collective-permute-start(bf16[128,2048]{1,0:T(8,128)(2,1)S(1)} %multiply_convert_fusion.10), channel_id=1, source_target_pairs={{0,2},{1,3},{2,0},{3,1},{4,6},{5,7},{6,4},{7,5},{8,10},{9,11},{10,... | collective-permute-start | bytes 1572872 | tf_op jit(solution)/shard_map/ppermute | solution.py:24
  317.9 366.6 %collective-permute-start.42 = (bf16[3,4,128,2048]{3,2,1,0:T(8,128)(2,1)}, bf16[3,4,128,2048]{3,2,1,0:T(8,128)(2,1)}, u32[]{:S(2)}, u32[]{:S(2)}) collective-permute-start(bf16[3,4,128,2048]{3,2,1,0:T(8,128)(2,1)} %get-tuple-element.38), channel_id=1, source_target_pairs={{0,1},{1,0},{2,3},{3,2},{4,5},{5,4},{6,7},{7,6},{8,9},{9,8},{10,11... | collective-permute-start | bytes 18874376 | tf_op jit(solution)/shard_map/ppermute | solution.py:24
  319.8 137.4 %collective-permute-start.28 = (bf16[4,128,2048]{2,1,0:T(8,128)(2,1)S(1)}, bf16[4,128,2048]{2,1,0:T(8,128)(2,1)S(1)}, u32[]{:S(2)}, u32[]{:S(2)}) collective-permute-start(bf16[4,128,2048]{2,1,0:T(8,128)(2,1)S(1)} %get-tuple-element.63), channel_id=1, source_target_pairs={{0,16},{8,24},{16,0},{24,8},{1,17},{9,25},{17,1},{25,9},{2,18},{10... | collective-permute-start | bytes 6291464 | tf_op jit(solution)/shard_map/ppermute | solution.py:24
  365.3 137.3 %collective-permute-start.27 = (bf16[4,128,2048]{2,1,0:T(8,128)(2,1)S(1)}, bf16[4,128,2048]{2,1,0:T(8,128)(2,1)S(1)}, u32[]{:S(2)}, u32[]{:S(2)}) collective-permute-start(bf16[4,128,2048]{2,1,0:T(8,128)(2,1)S(1)} %get-tuple-element.63), channel_id=1, source_target_pairs={{0,8},{8,0},{16,24},{24,16},{1,9},{9,1},{17,25},{25,17},{2,10},{10... | collective-permute-start | bytes 6291464 | tf_op jit(solution)/shard_map/ppermute | solution.py:24
  365.3 137.4 %collective-permute-start.29 = (bf16[4,128,2048]{2,1,0:T(8,128)(2,1)S(1)}, bf16[4,128,2048]{2,1,0:T(8,128)(2,1)S(1)}, u32[]{:S(2)}, u32[]{:S(2)}) collective-permute-start(bf16[4,128,2048]{2,1,0:T(8,128)(2,1)S(1)} %get-tuple-element.63), channel_id=1, source_target_pairs={{0,24},{8,16},{16,8},{24,0},{1,25},{9,17},{17,9},{25,1},{2,26},{10... | collective-permute-start | bytes 6291464 | tf_op jit(solution)/shard_map/ppermute | solution.py:24
  367.0 153.0 %collective-permute-start.16 = (f32[2,16,128]{2,1,0:T(8,128)S(1)}, f32[2,16,128]{2,1,0:T(8,128)S(1)}, u32[]{:S(2)}, u32[]{:S(2)}) collective-permute-start(f32[2,16,128]{2,1,0:T(8,128)S(1)} %get-tuple-element.93), channel_id=1, source_target_pairs={{0,4},{1,5},{2,6},{3,7},{4,0},{5,1},{6,2},{7,3},{8,12},{9,13},{10,... | collective-permute-start | bytes 49160 | tf_op jit(solution)/shard_map/ppermute | solution.py:24
  457.2 65.7 %collective-permute-start.15 = (f32[2,16,128]{2,1,0:T(8,128)S(1)}, f32[2,16,128]{2,1,0:T(8,128)S(1)}, u32[]{:S(2)}, u32[]{:S(2)}) collective-permute-start(f32[2,16,128]{2,1,0:T(8,128)S(1)} %get-tuple-element.93), channel_id=1, source_target_pairs={{0,2},{1,3},{2,0},{3,1},{4,6},{5,7},{6,4},{7,5},{8,10},{9,11},{10,... | collective-permute-start | bytes 49160 | tf_op jit(solution)/shard_map/ppermute | solution.py:24
  502.7 173.4 %collective-permute-start.38 = (bf16[4,128,2048]{2,1,0:T(8,128)(2,1)}, bf16[4,128,2048]{2,1,0:T(8,128)(2,1)}, u32[]{:S(2)}, u32[]{:S(2)}) collective-permute-start(bf16[4,128,2048]{2,1,0:T(8,128)(2,1)} %get-tuple-element.58), channel_id=1, source_target_pairs={{0,1},{1,0},{2,3},{3,2},{4,5},{5,4},{6,7},{7,6},{8,9},{9,8},{10,11... | collective-permute-start | bytes 6291464 | tf_op jit(solution)/shard_map/ppermute | solution.py:24
  508.1 205.4 %collective-permute-start.30 = (bf16[3,4,128,2048]{3,2,1,0:T(8,128)(2,1)}, bf16[3,4,128,2048]{3,2,1,0:T(8,128)(2,1)}, u32[]{:S(2)}, u32[]{:S(2)}) collective-permute-start(bf16[3,4,128,2048]{3,2,1,0:T(8,128)(2,1)} %get-tuple-element.42), channel_id=1, source_target_pairs={{0,1},{1,0},{2,3},{3,2},{4,5},{5,4},{6,7},{7,6},{8,9},{9,8},{10,11... | collective-permute-start | bytes 18874376 | tf_op jit(solution)/shard_map/ppermute | solution.py:24
  515.0 217.1 %all-to-all-start.2 = ((bf16[8,256,2048]{2,1,0:T(8,128)(2,1)}), bf16[8,256,2048]{2,1,0:T(8,128)(2,1)}, u32[]{:S(2)}, u32[]{:S(2)}) async-start(bf16[8,256,2048]{2,1,0:T(8,128)(2,1)} %get-tuple-element.30), calls=%async_computation.2 | async-start | bytes 16777216 | tf_op jit(solution)/shard_map/all_to_all | solution.py:72
  520.0 94.3 %collective-permute-start.17 = (f32[2,16,128]{2,1,0:T(8,128)S(1)}, f32[2,16,128]{2,1,0:T(8,128)S(1)}, u32[]{:S(2)}, u32[]{:S(2)}) collective-permute-start(f32[2,16,128]{2,1,0:T(8,128)S(1)} %get-tuple-element.93), channel_id=1, source_target_pairs={{0,6},{1,7},{2,4},{3,5},{4,2},{5,3},{6,0},{7,1},{8,14},{9,15},{10,... | collective-permute-start | bytes 49160 | tf_op jit(solution)/shard_map/ppermute | solution.py:24
  522.9 157.4 %collective-permute-start.26 = (bf16[4,128,2048]{2,1,0:T(8,128)(2,1)}, bf16[4,128,2048]{2,1,0:T(8,128)(2,1)}, u32[]{:S(2)}, u32[]{:S(2)}) collective-permute-start(bf16[4,128,2048]{2,1,0:T(8,128)(2,1)} %copy-done.26), channel_id=1, source_target_pairs={{0,1},{1,0},{2,3},{3,2},{4,5},{5,4},{6,7},{7,6},{8,9},{9,8},{10,11... | collective-permute-start | bytes 6291464 | tf_op jit(solution)/shard_map/ppermute | solution.py:24
  614.3 45.2 %collective-permute-start.20 = (f32[4,2,16,128]{3,2,1,0:T(8,128)S(1)}, f32[4,2,16,128]{3,2,1,0:T(8,128)S(1)}, u32[]{:S(2)}, u32[]{:S(2)}) collective-permute-start(f32[4,2,16,128]{3,2,1,0:T(8,128)S(1)} %get-tuple-element.89), channel_id=1, source_target_pairs={{0,16},{8,24},{16,0},{24,8},{1,17},{9,25},{17,1},{25,9},{2,18},{10... | collective-permute-start | bytes 196616 | tf_op jit(solution)/shard_map/ppermute | solution.py:24
  732.1 99.2 %all-to-all-start.4 = ((bf16[8,256,2048]{2,1,0:T(8,128)(2,1)}), bf16[8,256,2048]{2,1,0:T(8,128)(2,1)}, u32[]{:S(2)}, u32[]{:S(2)}) async-start(bf16[8,256,2048]{2,1,0:T(8,128)(2,1)} %get-tuple-element.29), calls=%async_computation.4 | async-start | bytes 16777216 | tf_op jit(solution)/shard_map/all_to_all | solution.py:72
  831.3 53.9 %all-to-all-start.5 = ((bf16[8,256,1024]{2,1,0:T(8,128)(2,1)}), bf16[8,256,1024]{2,1,0:T(8,128)(2,1)}, u32[]{:S(2)}, u32[]{:S(2)}) async-start(bf16[8,256,1024]{2,1,0:T(8,128)(2,1)} %get-tuple-element.31), calls=%async_computation.5 | async-start | bytes 8388608 | tf_op jit(solution)/shard_map/all_to_all | solution.py:72
  939.0 77.4 %all-to-all-start.11 = ((bf16[8,256,1024]{2,1,0:T(8,128)(2,1)}), bf16[8,256,1024]{2,1,0:T(8,128)(2,1)}, u32[]{:S(2)}, u32[]{:S(2)}) async-start(bf16[8,256,1024]{2,1,0:T(8,128)(2,1)} %bitcast.348), calls=%async_computation.11 | async-start | bytes 8388608 | tf_op jit(solution)/shard_map/all_to_all | solution.py:72
  946.4 57.1 %collective-permute-start.44 = (bf16[128,2048]{1,0:T(8,128)(2,1)S(1)}, bf16[128,2048]{1,0:T(8,128)(2,1)S(1)}, u32[]{:S(2)}, u32[]{:S(2)}) collective-permute-start(bf16[128,2048]{1,0:T(8,128)(2,1)S(1)} %get-tuple-element.54), channel_id=1, source_target_pairs={{0,2},{1,3},{2,0},{3,1},{4,6},{5,7},{6,4},{7,5},{8,10},{9,11},{10,... | collective-permute-start | bytes 1572872 | tf_op jit(solution)/shard_map/ppermute | solution.py:24
  948.4 66.8 %collective-permute-start.46 = (bf16[128,2048]{1,0:T(8,128)(2,1)S(1)}, bf16[128,2048]{1,0:T(8,128)(2,1)S(1)}, u32[]{:S(2)}, u32[]{:S(2)}) collective-permute-start(bf16[128,2048]{1,0:T(8,128)(2,1)S(1)} %get-tuple-element.55), channel_id=1, source_target_pairs={{0,6},{1,7},{2,4},{3,5},{4,2},{5,3},{6,0},{7,1},{8,14},{9,15},{10,... | collective-permute-start | bytes 1572872 | tf_op jit(solution)/shard_map/ppermute | solution.py:24
  949.9 65.4 %collective-permute-start.45 = (bf16[128,2048]{1,0:T(8,128)(2,1)S(1)}, bf16[128,2048]{1,0:T(8,128)(2,1)S(1)}, u32[]{:S(2)}, u32[]{:S(2)}) collective-permute-start(bf16[128,2048]{1,0:T(8,128)(2,1)S(1)} %get-tuple-element.56), channel_id=1, source_target_pairs={{0,4},{1,5},{2,6},{3,7},{4,0},{5,1},{6,2},{7,3},{8,12},{9,13},{10,... | collective-permute-start | bytes 1572872 | tf_op jit(solution)/shard_map/ppermute | solution.py:24
  1016.4 84.4 %all-to-all-start.12 = ((bf16[8,256,1024]{2,1,0:T(8,128)(2,1)}), bf16[8,256,1024]{2,1,0:T(8,128)(2,1)}, u32[]{:S(2)}, u32[]{:S(2)}) async-start(bf16[8,256,1024]{2,1,0:T(8,128)(2,1)} %bitcast.347), calls=%async_computation.12 | async-start | bytes 8388608 | tf_op jit(solution)/shard_map/all_to_all | solution.py:72
  1022.5 59.3 %collective-permute-start.49 = (bf16[128,2048]{1,0:T(8,128)(2,1)S(1)}, bf16[128,2048]{1,0:T(8,128)(2,1)S(1)}, u32[]{:S(2)}, u32[]{:S(2)}) collective-permute-start(bf16[128,2048]{1,0:T(8,128)(2,1)S(1)} %fusion.142), channel_id=1, source_target_pairs={{0,6},{1,7},{2,4},{3,5},{4,2},{5,3},{6,0},{7,1},{8,14},{9,15},{10,... | collective-permute-start | bytes 1572872 | tf_op jit(solution)/shard_map/ppermute | solution.py:24
  1025.3 66.2 %collective-permute-start.48 = (bf16[128,2048]{1,0:T(8,128)(2,1)S(1)}, bf16[128,2048]{1,0:T(8,128)(2,1)S(1)}, u32[]{:S(2)}, u32[]{:S(2)}) collective-permute-start(bf16[128,2048]{1,0:T(8,128)(2,1)S(1)} %fusion.142), channel_id=1, source_target_pairs={{0,4},{1,5},{2,6},{3,7},{4,0},{5,1},{6,2},{7,3},{8,12},{9,13},{10,... | collective-permute-start | bytes 1572872 | tf_op jit(solution)/shard_map/ppermute | solution.py:24
  1025.9 65.7 %collective-permute-start.47 = (bf16[128,2048]{1,0:T(8,128)(2,1)S(1)}, bf16[128,2048]{1,0:T(8,128)(2,1)S(1)}, u32[]{:S(2)}, u32[]{:S(2)}) collective-permute-start(bf16[128,2048]{1,0:T(8,128)(2,1)S(1)} %fusion.142), channel_id=1, source_target_pairs={{0,2},{1,3},{2,0},{3,1},{4,6},{5,7},{6,4},{7,5},{8,10},{9,11},{10,... | collective-permute-start | bytes 1572872 | tf_op jit(solution)/shard_map/ppermute | solution.py:24
  1100.8 30.7 %all-to-all-start.8 = ((bf16[4,64,2048]{2,1,0:T(8,128)(2,1)}), bf16[4,64,2048]{2,1,0:T(8,128)(2,1)S(1)}, u32[]{:S(2)}, u32[]{:S(2)}) async-start(bf16[4,64,2048]{2,1,0:T(8,128)(2,1)} %bitcast.142), calls=%async_computation.8 | async-start | bytes 2097152 | tf_op jit(solution)/shard_map/all_to_all | solution.py:308
  1132.5 118.2 %all-to-all-start.9 = ((bf16[8,256,2048]{2,1,0:T(8,128)(2,1)}), bf16[8,256,2048]{2,1,0:T(8,128)(2,1)}, u32[]{:S(2)}, u32[]{:S(2)}) async-start(bf16[8,256,2048]{2,1,0:T(8,128)(2,1)} %bitcast.344), calls=%async_computation.9 | async-start | bytes 16777216 | tf_op jit(solution)/shard_map/all_to_all | solution.py:72
  1153.5 77.3 %collective-permute-start.52 = (f32[2,2,2,2,128]{4,3,2,1,0:T(2,128)S(1)}, f32[2,2,2,2,128]{4,3,2,1,0:T(2,128)S(1)}, u32[]{:S(2)}, u32[]{:S(2)}) collective-permute-start(f32[2,2,2,2,128]{4,3,2,1,0:T(2,128)S(1)} %reverse_add_fusion), channel_id=1, source_target_pairs={{0,2},{1,3},{2,0},{3,1},{4,6},{5,7},{6,4},{7,5},{8,10},{9,11},{10,... | collective-permute-start | bytes 24584 | tf_op jit(solution)/shard_map/ppermute | solution.py:24
  1250.7 75.8 %all-to-all-start.7 = ((bf16[32,64,768]{2,1,0:T(8,128)(2,1)}), bf16[32,64,768]{2,1,0:T(8,128)(2,1)}, u32[]{:S(2)}, u32[]{:S(2)}) async-start(bf16[32,64,768]{2,1,0:T(8,128)(2,1)} %bitcast.334), calls=%async_computation.7 | async-start | bytes 6291456 | tf_op jit(solution)/shard_map/all_to_all | solution.py:294
  1326.5 99.7 %all-to-all-start.10 = ((bf16[8,256,2048]{2,1,0:T(8,128)(2,1)}), bf16[8,256,2048]{2,1,0:T(8,128)(2,1)}, u32[]{:S(2)}, u32[]{:S(2)}) async-start(bf16[8,256,2048]{2,1,0:T(8,128)(2,1)} %bitcast.345), calls=%async_computation.10 | async-start | bytes 16777216 | tf_op jit(solution)/shard_map/all_to_all | solution.py:72
  1331.6 165.6 %all-gather.5.cloned.1.call-start = ((), (), s32[]{:S(2)}) async-start(), calls=%async_computation.14 | async-start | bytes 1310720 | tf_op jit(solution)/shard_map/all_gather | solution.py:312
  1347.0 153.0 %all-gather.3.cloned.1.call-start = ((), (), s32[]{:S(2)}) async-start(), calls=%async_computation.13 | async-start | bytes 3932160 | tf_op jit(solution)/shard_map/all_gather | solution.py:307
  1354.5 38.8 %collective-permute-start.54 = (bf16[4,128,2048]{2,1,0:T(8,128)(2,1)}, bf16[4,128,2048]{2,1,0:T(8,128)(2,1)}, u32[]{:S(2)}, u32[]{:S(2)}) collective-permute-start(bf16[4,128,2048]{2,1,0:T(8,128)(2,1)} %slice.324), channel_id=1, source_target_pairs={{0,1},{1,0},{2,3},{3,2},{4,5},{5,4},{6,7},{7,6},{8,9},{9,8},{10,11... | collective-permute-start | bytes 6291464 | tf_op jit(solution)/shard_map/ppermute | solution.py:24
  1363.0 115.0 %collective-permute-start.32 = (bf16[128,2048]{1,0:T(8,128)(2,1)}, bf16[128,2048]{1,0:T(8,128)(2,1)}, u32[]{:S(2)}, u32[]{:S(2)}) collective-permute-start(bf16[128,2048]{1,0:T(8,128)(2,1)} %get-tuple-element.59), channel_id=1, source_target_pairs={{0,2},{1,3},{2,0},{3,1},{4,6},{5,7},{6,4},{7,5},{8,10},{9,11},{10,... | collective-permute-start | bytes 1572872 | tf_op jit(solution)/shard_map/ppermute | solution.py:24
  1364.7 113.3 %collective-permute-start.34 = (bf16[128,2048]{1,0:T(8,128)(2,1)}, bf16[128,2048]{1,0:T(8,128)(2,1)}, u32[]{:S(2)}, u32[]{:S(2)}) collective-permute-start(bf16[128,2048]{1,0:T(8,128)(2,1)} %get-tuple-element.60), channel_id=1, source_target_pairs={{0,6},{1,7},{2,4},{3,5},{4,2},{5,3},{6,0},{7,1},{8,14},{9,15},{10,... | collective-permute-start | bytes 1572872 | tf_op jit(solution)/shard_map/ppermute | solution.py:24
  1399.6 59.3 %collective-permute-start.55 = (bf16[128,2048]{1,0:T(8,128)(2,1)}, bf16[128,2048]{1,0:T(8,128)(2,1)}, u32[]{:S(2)}, u32[]{:S(2)}) collective-permute-start(bf16[128,2048]{1,0:T(8,128)(2,1)} %get-tuple-element.49), channel_id=1, source_target_pairs={{0,2},{1,3},{2,0},{3,1},{4,6},{5,7},{6,4},{7,5},{8,10},{9,11},{10,... | collective-permute-start | bytes 1572872 | tf_op jit(solution)/shard_map/ppermute | solution.py:24
  1401.2 69.6 %collective-permute-start.57 = (bf16[128,2048]{1,0:T(8,128)(2,1)}, bf16[128,2048]{1,0:T(8,128)(2,1)}, u32[]{:S(2)}, u32[]{:S(2)}) collective-permute-start(bf16[128,2048]{1,0:T(8,128)(2,1)} %get-tuple-element.50), channel_id=1, source_target_pairs={{0,6},{1,7},{2,4},{3,5},{4,2},{5,3},{6,0},{7,1},{8,14},{9,15},{10,... | collective-permute-start | bytes 1572872 | tf_op jit(solution)/shard_map/ppermute | solution.py:24
  1401.5 69.3 %collective-permute-start.56 = (bf16[128,2048]{1,0:T(8,128)(2,1)}, bf16[128,2048]{1,0:T(8,128)(2,1)}, u32[]{:S(2)}, u32[]{:S(2)}) collective-permute-start(bf16[128,2048]{1,0:T(8,128)(2,1)} %get-tuple-element.51), channel_id=1, source_target_pairs={{0,4},{1,5},{2,6},{3,7},{4,0},{5,1},{6,2},{7,3},{8,12},{9,13},{10,... | collective-permute-start | bytes 1572872 | tf_op jit(solution)/shard_map/ppermute | solution.py:24
  (120 other events, 3250.7 us)
Sparse Core Ops, SparseCore 0:
  1347.1 27.7 all-gather.4
  1382.6 62.2 all-gather.2
